TPU v7x, 32 devices: a whole 2x2x4 slice. The times are simulated.
32 devices in a mesh: grp: 4 (over y, x), seq: 4 (over z), mlp: 2 (over core).
Axes of the slice: x: 2, y: 2, z: 4, core: 2. Of those that a mesh axis runs over, the one named last changes fastest.
Arguments:
- queries: bfloat16 [16, 4, 4096], P('grp'), may hold values from -6 to 6
- new_keys: bfloat16 [16, 4, 4096], P(('grp', 'seq')), may hold values from -6 to 6
- new_values: bfloat16 [16, 4, 4096], P(('grp', 'seq')), may hold values from -6 to 6
- prefix_keys: bfloat16 [4, 2048, 4096], P('grp', ('seq', 'mlp')), may hold values from -250 to 250
- prefix_values: bfloat16 [4, 2048, 4096], P('grp', ('seq', 'mlp')), may hold values from -6 to 6
- tail_keys: bfloat16 [16, 256, 4096], P(('grp', 'seq'), 'mlp'), may hold values from -6 to 6
- tail_values: bfloat16 [16, 256, 4096], P(('grp', 'seq'), 'mlp'), may hold values from -6 to 6
- prefix_len: int32 [4], P('grp'), may hold values from 1 to 2048, as said below
- tail_len: int32 [16], P('grp'), may hold values from 0 to 256, as said below
- resid: bfloat16 [16, 4, 4096], P('grp', None, ('seq', 'mlp')), may hold values from -12 to 12
- w_out: bfloat16 [4096, 4096], P(None, ('seq', 'mlp')), may hold values from -0.09375 to 0.09375
- ln_gain: bfloat16 [4096], P(('seq', 'mlp')), may hold values from 0.25 to 1.75
- w_up: bfloat16 [4096, 16384], P(('seq', 'mlp'), 'grp'), may hold values from -0.09375 to 0.09375
- w_down: bfloat16 [16384, 4096], P('grp', ('seq', 'mlp')), may hold values from -0.046875 to 0.046875
Outputs:
- out: float32 [16, 4, 4096], P('grp', None, ('seq', 'mlp'))
Inputs may be any that keep to these rules, and one draw needn't show every extreme that they name: `prefix_len`: every group's live prefix is 1 to 2048 slots; in every draw some group's prefix fills all 2048 slots. `tail_len`: A request's live tail is 0 to 256 slots; in every draw some request's tail fills all 256 slots.
All inputs are finite; a program needn't handle non-finite values.
Results may differ from a plain program's by a relative error of at most 0.0075.
Values may be sent and summed in bfloat16 or wider, within the bound.
A program may use at most 128 MiB of HBM per device.

v0:
```python
import math
import jax
import jax.numpy as jnp
from jax import lax
from jax.sharding import PartitionSpec as P

D = 4096
H = 32
NEG = -1e30


def merged(value, axis, join):
    pieces = jax.tree.map(lambda part: lax.all_gather(part, axis), value)
    head = jax.tree.map(lambda part: part[0], pieces)
    tail = jax.tree.map(lambda part: part[1:], pieces)
    so_far, _ = lax.scan(lambda so_far, piece: (join(so_far, piece), None), head, tail)
    return so_far


def head_slopes(count):
    return jnp.power(2.0, -8.0 * (jnp.arange(count, dtype=jnp.float32) + 1.0) / count)


def attend(query_rows, key_block, value_block, query_pos, key_pos, key_mask):
    head_count = query_rows.shape[1]
    inv_scale = 1.0 / math.sqrt(query_rows.shape[2])
    scores = (
        jnp.einsum("qhd,khd->hqk", query_rows, key_block, preferred_element_type=jnp.float32)
        * inv_scale
    )
    distance = (query_pos[:, None] - key_pos[None, :]).astype(jnp.float32)
    scores = scores - head_slopes(head_count)[:, None, None] * distance[None, :, :]
    scores = jnp.where(key_mask, scores, NEG)
    row_max = jnp.max(scores, axis=2)
    weights = jnp.where(key_mask, jnp.exp(scores - row_max[:, :, None]), 0.0)
    weight_sum = jnp.sum(weights, axis=2)
    mixed_sum = jnp.einsum(
        "hqk,khd->qhd",
        weights.astype(jnp.bfloat16),
        value_block,
        preferred_element_type=jnp.float32,
    )
    return (row_max.T, weight_sum.T, mixed_sum)


def join_parts(first, second):
    best_max = jnp.maximum(first[0], second[0])
    factor_one = jnp.exp(first[0] - best_max)
    factor_two = jnp.exp(second[0] - best_max)
    return (
        best_max,
        first[1] * factor_one + second[1] * factor_two,
        first[2] * factor_one[:, :, None] + second[2] * factor_two[:, :, None],
    )


def body(
    queries,
    new_keys,
    new_values,
    prefix_keys,
    prefix_values,
    tail_keys,
    tail_values,
    prefix_len,
    tail_len,
    resid,
    w_out,
    ln_gain,
    w_up,
    w_down,
):
    group_req, step_count, model_width = queries.shape
    head_dim = model_width // H
    row_count = group_req * step_count
    seq_index = lax.axis_index("seq")
    core_index = lax.axis_index("mlp")
    block_len = prefix_keys.shape[1]
    tail_block = tail_keys.shape[1]
    block_start = (seq_index * lax.axis_size("mlp") + core_index) * block_len
    prefix_end = prefix_len[0]
    step_index = jnp.arange(step_count, dtype=jnp.int32)
    query_pos = prefix_end + jnp.repeat(tail_len, step_count) + jnp.tile(step_index, group_req)
    query_rows = queries.reshape(row_count, H, head_dim)
    key_pos = block_start + jnp.arange(block_len, dtype=jnp.int32)
    key_live = key_pos < prefix_end
    own_len = lax.dynamic_index_in_dim(tail_len, seq_index, 0, keepdims=False)
    own_rows = lax.dynamic_slice_in_dim(query_rows, seq_index * step_count, step_count, 0)
    own_pos = prefix_end + own_len + step_index
    tail_index = core_index * tail_block + jnp.arange(tail_block, dtype=jnp.int32)
    partial_value = attend(
        query_rows,
        prefix_keys[0].reshape(block_len, H, head_dim),
        prefix_values[0].reshape(block_len, H, head_dim),
        query_pos,
        key_pos,
        key_live[None, None, :],
    )
    tail_result = attend(
        own_rows,
        tail_keys[0].reshape(tail_block, H, head_dim),
        tail_values[0].reshape(tail_block, H, head_dim),
        own_pos,
        prefix_end + tail_index,
        (tail_index < own_len)[None, None, :],
    )
    self_mask = (step_index[None, :] <= step_index[:, None]) & (core_index == 0)
    self_result = attend(
        own_rows,
        new_keys[0].reshape(step_count, H, head_dim),
        new_values[0].reshape(step_count, H, head_dim),
        own_pos,
        own_pos,
        self_mask[None, :, :],
    )
    own_slice = tuple(
        (
            lax.dynamic_slice_in_dim(member, seq_index * step_count, step_count, 0)
            for member in partial_value
        )
    )
    own_part = join_parts(join_parts(own_slice, tail_result), self_result)
    partial_value = tuple(
        (
            lax.dynamic_update_slice_in_dim(member, update, seq_index * step_count, 0)
            for member, update in zip(partial_value, own_part)
        )
    )
    row_max, weight_sum, mixed_sum = merged(
        (partial_value[0], partial_value[1], partial_value[2]), ("seq", "mlp"), join_parts
    )
    attention = (
        (mixed_sum / weight_sum[:, :, None]).astype(jnp.bfloat16).reshape(row_count, model_width)
    )
    width_block = resid.shape[2]
    stream = resid.astype(jnp.float32).reshape(row_count, width_block) + jnp.dot(
        attention, w_out, preferred_element_type=jnp.float32
    )
    row_sums, squares = lax.psum(
        (jnp.sum(stream, axis=1), jnp.sum(stream * stream, axis=1)), ("seq", "mlp")
    )
    row_mean = row_sums / D
    row_var = squares / D - row_mean * row_mean
    hidden = (
        (stream - row_mean[:, None])
        * lax.rsqrt(row_var[:, None] + 1e-05)
        * ln_gain.astype(jnp.float32)
    ).astype(jnp.bfloat16)
    lifted = jnp.dot(
        lax.all_gather(hidden, "grp", axis=0, tiled=True), w_up, preferred_element_type=jnp.float32
    )
    summed = lax.psum(lifted, ("seq", "mlp"))
    activated = jax.nn.gelu(summed, approximate=False).astype(jnp.bfloat16)
    projected = lax.psum_scatter(
        jnp.dot(activated, w_down, preferred_element_type=jnp.float32),
        "grp",
        scatter_dimension=0,
        tiled=True,
    )
    return (stream + projected).reshape(group_req, step_count, width_block)


def solution(mesh):
    return jax.shard_map(
        body,
        mesh=mesh,
        in_specs=(
            P("grp", None, None),
            P(("grp", "seq"), None, None),
            P(("grp", "seq"), None, None),
            P("grp", ("seq", "mlp"), None),
            P("grp", ("seq", "mlp"), None),
            P(("grp", "seq"), "mlp", None),
            P(("grp", "seq"), "mlp", None),
            P("grp"),
            P("grp"),
            P("grp", None, ("seq", "mlp")),
            P(None, ("seq", "mlp")),
            P(("seq", "mlp")),
            P(("seq", "mlp"), "grp"),
            P("grp", ("seq", "mlp")),
        ),
        out_specs=P("grp", None, ("seq", "mlp")),
        check_vma=False,
    )
```

profile of v0, /device:TPU:0, one launch (start us, length us, event | category | flops | bytes accessed | tf_op | source)
XLA Modules:
  0.0 181.5 jit_solution(5606925134826433128)
XLA Ops:
  7.4 1.2 dynamic_slice.28
  9.2 0.6 fusion.102
  9.9 1.1 reshape.182
  11.0 1.4 copy.98
  12.5 0.7 fusion.143
  14.4 1.2 fusion.142
  17.4 1.0 fusion.3
  19.1 0.5 fusion.22
  19.8 0.8 copy.92
  21.0 15.8 %all_gather.32 = f32[8,16,32]{2,1,0:T(8,128)S(1)} all-gather(f32[1,16,32]{2,1,0:T(8,128)S(1)} %copy.83), channel_id=1, replica_groups=mesh['grp'=4,'seq'=4,'mlp'=2] {'seq','mlp'}, dimensions={0}, use_global_device_ids=true | all-gather | bytes 18432 | tf_op jit(solution)/shard_map/all_gather | solution.py:13
  37.2 14.1 %all_gather.29 = f32[8,16,32]{2,1,0:T(8,128)S(1)} all-gather(f32[1,16,32]{2,1,0:T(8,128)S(1)} %copy.76), channel_id=1, replica_groups=mesh['grp'=4,'seq'=4,'mlp'=2] {'seq','mlp'}, dimensions={0}, use_global_device_ids=true | all-gather | bytes 18432 | tf_op jit(solution)/shard_map/all_gather | solution.py:13
  51.4 1.7 all-gather.2.cloned.1.call-done
  53.1 1.7 slice.29
  54.8 1.0 slice_bitcast_fusion
  55.8 2.2 %while.14 = (s32[]{:T(128)}, f32[16,32]{1,0:T(8,128)S(1)}, f32[16,32]{1,0:T(8,128)S(1)}, f32[16,32,128]{2,1,0:T(8,128)S(1)}, f32[7,16,32]{2,1,0:T(8,128)S(1)}, /...) while((s32[]{:T(128)}, f32[16,32]{1,0:T(8,128)S(1)}, f32[16,32]{1,0:T(8,128)S(1)}, ...), condition=%wide.region_7.8_spmd, body=%wide.region_6.7_spmd.sunk | while | flops 199682 | bytes 807005 | solution.py:16
  58.1 3.0 %fusion.137 = (f32[16]{0:T(128)S(1)}, f32[16]{0:T(128)S(1)}, f32[16,512]{1,0:T(8,128)S(1)}) fusion(f32[16,512]{1,0:T(8,128)S(1)} %reshape.186, bf16[4096,512]{1,0:T(8,128)(2,1)} %param.26, bf16[2,8,32,128]{3,2,1,0:T(8,128)(2,1)S(1)} %bitcast.177), kind=kOutput, calls=%fused_computation.181 | convolution fusion | flops 67141600 | bytes 4391040 | tf_op jit(solution)/shard_map/dot_general | solution.py:136
  61.1 15.5 %all-reduce = (f32[16]{0:T(128)S(1)}, f32[16]{0:T(128)S(1)}) all-reduce(f32[16]{0:T(128)S(1)} %get-tuple-element.60, f32[16]{0:T(128)S(1)} %get-tuple-element.59), channel_id=1, replica_groups=mesh['grp'=4,'seq'=4,'mlp'=2] {'seq','mlp'}, use_global_device_ids=true, to_apply=%region_11.12 | all-reduce | flops 32 | bytes 256 | tf_op jit(solution)/shard_map/psum | solution.py:139
  76.6 8.1 %all_gather.36 = bf16[64,512]{1,0:T(8,128)(2,1)S(1)} all-gather(bf16[16,512]{1,0:T(8,128)(2,1)S(1)} %multiply_convert_fusion), channel_id=1, replica_groups=mesh['grp'=4,'seq'=4,'mlp'=2] {'grp'}, dimensions={0}, use_global_device_ids=true | all-gather | bytes 81920 | tf_op jit(solution)/shard_map/all_gather | solution.py:150
  84.8 4.1 %fusion.144 = f32[64,4096]{1,0:T(8,128)} fusion(bf16[64,512]{1,0:T(8,128)(2,1)S(1)} %all_gather.36, bf16[512,4096]{1,0:T(8,128)(2,1)} %param.28), kind=kOutput, calls=%fused_computation.184 | convolution fusion | flops 268435456 | bytes 5308416 | tf_op jit(solution)/shard_map/dot_general | solution.py:149
  88.9 56.1 %all-reduce.3.cloned.1.call-done = f32[64,4096]{1,0:T(8,128)} async-done(((f32[64,4096]{1,0:T(8,128)}), f32[64,4096]{1,0:T(8,128)}) %all-reduce.3.cloned.1.call-update) | async-done | bytes 1048592 | tf_op jit(solution)/shard_map/psum | solution.py:152
  145.1 5.5 %fusion.37 = f32[64,512]{1,0:T(8,128)} fusion(bf16[4096,512]{1,0:T(8,128)(2,1)} %param.29, f32[64,4096]{1,0:T(8,128)} %all-reduce.3.cloned.1.call-done), kind=kOutput, calls=%fused_computation.49 | convolution fusion | flops 285474816 | bytes 5373952 | tf_op jit(solution)/shard_map/dot_general | solution.py:155
  150.6 22.9 %reduce-scatter.2.cloned.1.call-done = f32[16,512]{1,0:T(8,128)} async-done(((f32[64,512]{1,0:T(8,128)}), f32[16,512]{1,0:T(8,128)}) %reduce-scatter.2.cloned.1.call-update) | async-done | bytes 32784 | tf_op jit(solution)/shard_map/reduce_scatter | solution.py:154
  173.6 0.8 add.168
  174.3 0.6 reshape.184
  (85 shorter events, 6.9 us)
Async XLA Ops:
  6.5 13.1 %copy-start = (bf16[1,4,4096]{2,1,0:T(4,128)(2,1)S(1)}, bf16[1,4,4096]{2,1,0:T(4,128)(2,1)}, u32[]{:S(2)}) copy-start(bf16[1,4,4096]{2,1,0:T(4,128)(2,1)} %param.18) | copy-start | bytes 98308
  6.5 7.1 %copy-start.7 = (s32[4]{0:T(128)S(1)}, s32[4]{0:T(128)}, u32[]{:S(2)}) copy-start(s32[4]{0:T(128)} %param.24) | copy-start | bytes 52
  6.5 7.2 %copy-start.1 = (bf16[1,256,4096]{2,1,0:T(8,128)(2,1)S(1)}, bf16[1,256,4096]{2,1,0:T(8,128)(2,1)}, u32[]{:S(2)}) copy-start(bf16[1,256,4096]{2,1,0:T(8,128)(2,1)} %param.19) | copy-start | bytes 6291460
  6.5 46.6 %all-gather.2.cloned.1.call-start = ((), (), s32[]{:S(2)}) async-start(), calls=%async_computation.1 | async-start | bytes 2359296 | tf_op jit(solution)/shard_map/all_gather | solution.py:13
  14.3 1.8 copy-start.4
  14.3 2.6 %copy-start.2 = (bf16[1,256,4096]{2,1,0:T(8,128)(2,1)S(1)}, bf16[1,256,4096]{2,1,0:T(8,128)(2,1)}, u32[]{:S(2)}) copy-start(bf16[1,256,4096]{2,1,0:T(8,128)(2,1)} %param.20) | copy-start | bytes 6291460
  17.3 1.2 copy-start.3
  18.8 32.5 %copy-start.5 = (bf16[4,4,512]{2,1,0:T(4,128)(2,1)S(1)}, bf16[4,4,512]{2,1,0:T(4,128)(2,1)}, u32[]{:S(2)}) copy-start(bf16[4,4,512]{2,1,0:T(4,128)(2,1)} %param.25) | copy-start | bytes 49156
  18.8 32.5 %copy-start.6 = (bf16[512]{0:T(512)(128)(2,1)S(1)}, bf16[512]{0:T(512)(128)(2,1)}, u32[]{:S(2)}) copy-start(bf16[512]{0:T(512)(128)(2,1)} %param.27) | copy-start | bytes 3076
  20.6 124.4 %all-reduce.3.cloned.1.call-start = ((), (), s32[]{:S(2)}) async-start(), calls=%async_computation.2 | async-start | bytes 2097152 | tf_op jit(solution)/shard_map/psum | solution.py:152
  88.9 84.7 %reduce-scatter.2.cloned.1.call-start = ((), (), s32[]{:S(2)}) async-start(), calls=%async_computation.3 | async-start | bytes 163840 | tf_op jit(solution)/shard_map/reduce_scatter | solution.py:154
Sparse Core Ops, SparseCore 0:
  20.8 32.3 all-gather.1
  89.0 56.0 all-reduce.2
  150.7 22.7 reduce-scatter.1
where the time goes:
time: 182 us; the launch traced here: 181 us
  waiting for transfers between devices  80.9 us (44%)
  blocking collectives  53.5 us (29%)
  matrix products  16.5 us (9%)
  between operations  14.8 us (8%)
  local copies, waits for them, and re-layouts  11 us (6%)
  other arithmetic  4.55 us (2%)
    psum x1, waiting for transfers between devices, body(): summed = lax.psum(lifted, ('seq', 'mlp'))  56.1 us
    all_gather x2, blocking collectives, merged(): pieces = jax.tree.map(lambda part: lax.all_gather(part, axis), value)  29.9 us
    reduce_scatter x1, waiting for transfers between devices, body(): lax.psum_scatter(jnp.dot(activated, w_down, preferred_element_type=jnp.fl...  22.9 us
    psum x1, blocking collectives, body(): lax.psum((jnp.sum(stream, axis=1), jnp.sum(stream * stream, axis=1)), ('s...  15.5 us
    all_gather x1, blocking collectives, body(): lax.all_gather(hidden, 'grp', axis=0, tiled=True)  8.13 us
    dot_general x1, matrix products, body(): jnp.dot(activated, w_down, preferred_element_type=jnp.float32)  5.52 us
    dot_general x1, matrix products, body(): jnp.dot(lax.all_gather(hidden, 'grp', axis=0, tiled=True), w_up, preferre...  4.1 us
  transfers between devices with their start and end apart: 3, of which 3 were waited for; matrix products, arithmetic and copies ran while one was open for 0% of the time, Pallas kernels for 0%

commit v1 on v0

--- a/solution.py
+++ b/solution.py
@@ -149,7 +149,7 @@
     lifted = jnp.dot(
         lax.all_gather(hidden, "grp", axis=0, tiled=True), w_up, preferred_element_type=jnp.float32
     )
-    summed = lax.psum(lifted, ("seq", "mlp"))
+    summed = lax.psum(lax.psum(lifted, "mlp"), "seq")
     activated = jax.nn.gelu(summed, approximate=False).astype(jnp.bfloat16)
     projected = lax.psum_scatter(
         jnp.dot(activated, w_down, preferred_element_type=jnp.float32),

time: 182 us -> 199 us (1.093)
  waiting for transfers between devices: 80.9 us -> 97.6 us
    psum x1 -> x2, waiting for transfers between devices: 56.1 us -> 72.4 us  [body(): summed = lax.psum(lax.psum(lifted, 'mlp'), 'seq')]
  transfers between devices with their start and end apart: 3 -> 4, of which waited for: 3 -> 4; matrix products, arithmetic and copies ran while one was open for 0% -> 0% of each run, Pallas kernels for 0% -> 0%
where the time goes in v1:
time: 199 us; the launch traced here: 198 us
  waiting for transfers between devices  97.6 us (49%)
  blocking collectives  53.5 us (27%)
  matrix products  16.5 us (8%)
  between operations  14.8 us (7%)
  local copies, waits for them, and re-layouts  11 us (6%)
  other arithmetic  4.55 us (2%)
    psum x2, waiting for transfers between devices, body(): summed = lax.psum(lax.psum(lifted, 'mlp'), 'seq')  72.4 us
    all_gather x2, blocking collectives, merged(): pieces = jax.tree.map(lambda part: lax.all_gather(part, axis), value)  29.9 us
    reduce_scatter x1, waiting for transfers between devices, body(): lax.psum_scatter(jnp.dot(activated, w_down, preferred_element_type=jnp.fl...  23.4 us
    psum x1, blocking collectives, body(): lax.psum((jnp.sum(stream, axis=1), jnp.sum(stream * stream, axis=1)), ('s...  15.5 us
    all_gather x1, blocking collectives, body(): lax.all_gather(hidden, 'grp', axis=0, tiled=True)  8.13 us
    dot_general x1, matrix products, body(): jnp.dot(activated, w_down, preferred_element_type=jnp.float32)  5.51 us
    dot_general x1, matrix products, body(): jnp.dot(lax.all_gather(hidden, 'grp', axis=0, tiled=True), w_up, preferre...  4.1 us
  transfers between devices with their start and end apart: 4, of which 4 were waited for; matrix products, arithmetic and copies ran while one was open for 0% of the time, Pallas kernels for 0%

profile of v1, /device:TPU:0, one launch (start us, length us, event | category | flops | bytes accessed | tf_op | source)
XLA Modules:
  0.0 198.3 jit_solution(11466417132712250505)
XLA Ops:
  7.4 1.2 dynamic_slice.28
  9.2 0.6 fusion.102
  9.9 1.1 reshape.182
  11.0 1.4 copy.98
  12.5 0.7 fusion.143
  14.4 1.2 fusion.142
  17.4 1.0 fusion.3
  19.8 0.8 copy.92
  21.0 15.8 %all_gather.32 = f32[8,16,32]{2,1,0:T(8,128)S(1)} all-gather(f32[1,16,32]{2,1,0:T(8,128)S(1)} %copy.83), channel_id=1, replica_groups=mesh['grp'=4,'seq'=4,'mlp'=2] {'seq','mlp'}, dimensions={0}, use_global_device_ids=true | all-gather | bytes 18432 | tf_op jit(solution)/shard_map/all_gather | solution.py:13
  37.2 14.1 %all_gather.29 = f32[8,16,32]{2,1,0:T(8,128)S(1)} all-gather(f32[1,16,32]{2,1,0:T(8,128)S(1)} %copy.76), channel_id=1, replica_groups=mesh['grp'=4,'seq'=4,'mlp'=2] {'seq','mlp'}, dimensions={0}, use_global_device_ids=true | all-gather | bytes 18432 | tf_op jit(solution)/shard_map/all_gather | solution.py:13
  51.4 1.7 all-gather.2.cloned.1.call-done
  53.1 1.7 slice.29
  54.8 1.0 slice_bitcast_fusion
  55.8 2.2 %while.14 = (s32[]{:T(128)}, f32[16,32]{1,0:T(8,128)S(1)}, f32[16,32]{1,0:T(8,128)S(1)}, f32[16,32,128]{2,1,0:T(8,128)S(1)}, f32[7,16,32]{2,1,0:T(8,128)S(1)}, /...) while((s32[]{:T(128)}, f32[16,32]{1,0:T(8,128)S(1)}, f32[16,32]{1,0:T(8,128)S(1)}, ...), condition=%wide.region_7.8_spmd, body=%wide.region_6.7_spmd.sunk | while | flops 199682 | bytes 807005 | solution.py:16
  58.1 3.0 %fusion.137 = (f32[16]{0:T(128)S(1)}, f32[16]{0:T(128)S(1)}, f32[16,512]{1,0:T(8,128)S(1)}) fusion(f32[16,512]{1,0:T(8,128)S(1)} %reshape.186, bf16[4096,512]{1,0:T(8,128)(2,1)} %param.26, bf16[2,8,32,128]{3,2,1,0:T(8,128)(2,1)S(1)} %bitcast.177), kind=kOutput, calls=%fused_computation.181 | convolution fusion | flops 67141600 | bytes 4391040 | tf_op jit(solution)/shard_map/dot_general | solution.py:136
  61.1 15.5 %all-reduce = (f32[16]{0:T(128)S(1)}, f32[16]{0:T(128)S(1)}) all-reduce(f32[16]{0:T(128)S(1)} %get-tuple-element.60, f32[16]{0:T(128)S(1)} %get-tuple-element.59), channel_id=1, replica_groups=mesh['grp'=4,'seq'=4,'mlp'=2] {'seq','mlp'}, use_global_device_ids=true, to_apply=%region_11.12 | all-reduce | flops 32 | bytes 256 | tf_op jit(solution)/shard_map/psum | solution.py:139
  76.6 8.1 %all_gather.36 = bf16[64,512]{1,0:T(8,128)(2,1)S(1)} all-gather(bf16[16,512]{1,0:T(8,128)(2,1)S(1)} %multiply_convert_fusion), channel_id=1, replica_groups=mesh['grp'=4,'seq'=4,'mlp'=2] {'grp'}, dimensions={0}, use_global_device_ids=true | all-gather | bytes 81920 | tf_op jit(solution)/shard_map/all_gather | solution.py:150
  84.8 4.1 %fusion.144 = f32[64,4096]{1,0:T(8,128)} fusion(bf16[64,512]{1,0:T(8,128)(2,1)S(1)} %all_gather.36, bf16[512,4096]{1,0:T(8,128)(2,1)} %param.28), kind=kOutput, calls=%fused_computation.184 | convolution fusion | flops 268435456 | bytes 5308416 | tf_op jit(solution)/shard_map/dot_general | solution.py:149
  88.9 16.9 %all-reduce.4.cloned.1.call-done = f32[64,4096]{1,0:T(8,128)} async-done(((f32[64,4096]{1,0:T(8,128)}), f32[64,4096]{1,0:T(8,128)}) %all-reduce.4.cloned.1.call-update) | async-done | bytes 1048592 | tf_op jit(solution)/shard_map/psum | solution.py:152
  105.9 55.5 %all-reduce.6.cloned.1.call-done = f32[64,4096]{1,0:T(8,128)} async-done(((f32[64,4096]{1,0:T(8,128)}), f32[64,4096]{1,0:T(8,128)}) %all-reduce.6.cloned.1.call-update) | async-done | bytes 1048592 | tf_op jit(solution)/shard_map/psum | solution.py:152
  161.4 5.5 %fusion.37 = f32[64,512]{1,0:T(8,128)} fusion(bf16[4096,512]{1,0:T(8,128)(2,1)} %param.29, f32[64,4096]{1,0:T(8,128)} %all-reduce.6.cloned.1.call-done), kind=kOutput, calls=%fused_computation.49 | convolution fusion | flops 285474816 | bytes 5373952 | tf_op jit(solution)/shard_map/dot_general | solution.py:155
  166.9 23.4 %reduce-scatter.2.cloned.1.call-done = f32[16,512]{1,0:T(8,128)} async-done(((f32[64,512]{1,0:T(8,128)}), f32[16,512]{1,0:T(8,128)}) %reduce-scatter.2.cloned.1.call-update) | async-done | bytes 32784 | tf_op jit(solution)/shard_map/reduce_scatter | solution.py:154
  190.3 0.8 add.170
  191.1 0.6 reshape.184
  (88 shorter events, 7.5 us)
Async XLA Ops:
  6.5 13.1 %copy-start = (bf16[1,4,4096]{2,1,0:T(4,128)(2,1)S(1)}, bf16[1,4,4096]{2,1,0:T(4,128)(2,1)}, u32[]{:S(2)}) copy-start(bf16[1,4,4096]{2,1,0:T(4,128)(2,1)} %param.18) | copy-start | bytes 98308
  6.5 7.1 %copy-start.7 = (s32[4]{0:T(128)S(1)}, s32[4]{0:T(128)}, u32[]{:S(2)}) copy-start(s32[4]{0:T(128)} %param.24) | copy-start | bytes 52
  6.5 7.2 %copy-start.1 = (bf16[1,256,4096]{2,1,0:T(8,128)(2,1)S(1)}, bf16[1,256,4096]{2,1,0:T(8,128)(2,1)}, u32[]{:S(2)}) copy-start(bf16[1,256,4096]{2,1,0:T(8,128)(2,1)} %param.19) | copy-start | bytes 6291460
  6.5 46.6 %all-gather.2.cloned.1.call-start = ((), (), s32[]{:S(2)}) async-start(), calls=%async_computation.1 | async-start | bytes 2359296 | tf_op jit(solution)/shard_map/all_gather | solution.py:13
  14.3 1.8 copy-start.4
  14.3 2.6 %copy-start.2 = (bf16[1,256,4096]{2,1,0:T(8,128)(2,1)S(1)}, bf16[1,256,4096]{2,1,0:T(8,128)(2,1)}, u32[]{:S(2)}) copy-start(bf16[1,256,4096]{2,1,0:T(8,128)(2,1)} %param.20) | copy-start | bytes 6291460
  17.3 1.2 copy-start.3
  18.8 32.5 %copy-start.5 = (bf16[4,4,512]{2,1,0:T(4,128)(2,1)S(1)}, bf16[4,4,512]{2,1,0:T(4,128)(2,1)}, u32[]{:S(2)}) copy-start(bf16[4,4,512]{2,1,0:T(4,128)(2,1)} %param.25) | copy-start | bytes 49156
  18.8 32.5 %copy-start.6 = (bf16[512]{0:T(512)(128)(2,1)S(1)}, bf16[512]{0:T(512)(128)(2,1)}, u32[]{:S(2)}) copy-start(bf16[512]{0:T(512)(128)(2,1)} %param.27) | copy-start | bytes 3076
  20.6 85.2 %all-reduce.4.cloned.1.call-start = ((), (), s32[]{:S(2)}) async-start(), calls=%async_computation.2 | async-start | bytes 2097152 | tf_op jit(solution)/shard_map/psum | solution.py:152
  88.9 72.5 %all-reduce.6.cloned.1.call-start = ((), (), s32[]{:S(2)}) async-start(), calls=%async_computation.3 | async-start | bytes 2097152 | tf_op jit(solution)/shard_map/psum | solution.py:152
  105.9 84.4 %reduce-scatter.2.cloned.1.call-start = ((), (), s32[]{:S(2)}) async-start(), calls=%async_computation.4 | async-start | bytes 163840 | tf_op jit(solution)/shard_map/reduce_scatter | solution.py:154
Sparse Core Ops, SparseCore 0:
  20.8 32.3 all-gather.1
  89.0 16.8 all-reduce.3
  108.4 52.9 all-reduce.5
  167.1 23.2 reduce-scatter.1
